TPU v7x, 256 devices: a whole 4x4x8 slice. The times are simulated.
256 devices in a mesh: tm: 16 (over x, y), space: 16 (over z, core).
Axes of the slice: x: 4, y: 4, z: 8, core: 2. Of those that a mesh axis runs over, the one named last changes fastest.
Arguments:
- queries: bfloat16 [32, 32, 32, 2240], P('tm', 'space'), may hold values from -6 to 6
- keys: bfloat16 [32, 32, 32, 2240], P('tm', 'space'), may hold values from -6 to 6
- values: bfloat16 [32, 32, 32, 2240], P('tm', 'space'), may hold values from -6 to 6
- out_grad: bfloat16 [32, 32, 32, 2240], P('tm', 'space'), may hold values from -6 to 6
- block_start: int32 [32], P('tm'), may hold values 0 or 1
- conv_input: bfloat16 [32, 32, 32, 5632], P('tm', 'space'), may hold values from -6 to 6
- conv_grad: bfloat16 [32, 32, 32, 5632], P('tm', 'space'), may hold values from -6 to 6
- conv_weight: float32 [9, 5632], replicated, may hold values from -2 to 2
Outputs:
- query_grad: bfloat16 [32, 32, 32, 2240], P('tm', 'space')
- key_grad: bfloat16 [32, 32, 32, 2240], P('tm', 'space')
- value_grad: bfloat16 [32, 32, 32, 2240], P('tm', 'space')
- input_grad: bfloat16 [32, 32, 32, 5632], P('tm', 'space')
- kernel_grad: float32 [9, 5632], replicated
All inputs are finite; a program needn't handle non-finite values. No bound on the sum of `block_start` on one device may be relied on, other than what follows from the above.
Results may differ from a plain program's by a relative error of at most 0.0088.
Values may be sent and summed in bfloat16 or wider, within the bound.
A program may use at most 128 MiB of HBM per device.

v0:
```python
import math

import jax
import jax.numpy as jnp
from jax import lax
from jax.sharding import PartitionSpec as P

HEADS = 20
HD = 112


highest = lax.Precision.HIGHEST


def with_halo(cells, sides, width):
    for axis, dim in sides:
        count = lax.axis_size(axis)
        ends = count - 1
        head = lax.slice_in_dim(cells, 0, width, axis=dim)
        tail = lax.slice_in_dim(cells, cells.shape[dim] - width, cells.shape[dim], axis=dim)
        cells = jnp.concatenate(
            [
                lax.ppermute(tail, axis, [(i, (i + 1) % count) for i in range(ends)]),
                cells,
                lax.ppermute(head, axis, [((i + 1) % count, i) for i in range(ends)]),
            ],
            axis=dim,
        )
    return cells


def prefix(part, axis, combine, identity, reverse):
    count = lax.axis_size(axis)
    place = lax.axis_index(axis)
    ahead = count - 1 - place if reverse else place
    gathered = jax.tree.map(lambda a: lax.all_gather(a, axis), part)
    state = jax.tree.map(lambda a, e: jnp.zeros_like(a) + jnp.asarray(e, a.dtype), part, identity)

    def one(turn, state):
        source = count - 1 - turn if reverse else turn
        return combine(
            state, jax.tree.map(lambda a: lax.dynamic_index_in_dim(a, source, 0, False), gathered)
        )

    return lax.fori_loop(0, ahead, one, state)


def lifted(x):
    widened = x.astype(jnp.float32)
    return jnp.where(widened > 0, widened + 1.0, jnp.exp(jnp.minimum(widened, 0.0)))


def slopes(x):
    widened = x.astype(jnp.float32)
    return jnp.where(widened > 0, 1.0, jnp.exp(jnp.minimum(widened, 0.0)))


def visibility(block_start, count):
    position = jnp.arange(count, dtype=jnp.int32)
    starts = jnp.where(position == 0, 1, block_start)
    block_ids = jnp.cumsum(starts)
    return (block_ids[None, :] <= block_ids[:, None]).astype(jnp.float32)


def add_pair(earlier, later):
    return (earlier[0] + later[0], earlier[1] + later[1])


def body(queries, keys, values, out_grad, block_start, conv_input, conv_grad, conv_weight):
    frames, rows, cols, width = queries.shape
    heads = HEADS
    depth = HD
    head_shape = (frames, rows * cols, heads, depth)
    q_feat = lifted(queries).astype(jnp.bfloat16).reshape(head_shape)
    k_feat = lifted(keys).astype(jnp.bfloat16).reshape(head_shape)
    v_heads = values.reshape(head_shape)
    visible = visibility(block_start, frames)
    rimmed = with_halo(conv_grad, (("space", 1),), 1)
    states = jnp.einsum("fnhd,fnhe->fhde", k_feat, v_heads, preferred_element_type=jnp.float32)
    sums = jnp.sum(k_feat.astype(jnp.float32), axis=1)
    states, sums = lax.psum((states, sums), "space")
    earlier = prefix(
        (jnp.sum(states, axis=0), jnp.sum(sums, axis=0)),
        "tm",
        add_pair,
        (jnp.zeros(states.shape[1:], jnp.float32), jnp.zeros(sums.shape[1:], jnp.float32)),
        False,
    )
    seen_states = jnp.einsum("fg,ghde->fhde", visible, states, precision=highest) + earlier[0][None]
    seen_sums = jnp.einsum("fg,ghd->fhd", visible, sums, precision=highest) + earlier[1][None]
    q_wide = q_feat.astype(jnp.float32)
    grad_wide = out_grad.reshape(head_shape).astype(jnp.float32)
    numer = jnp.einsum("fnhd,fhde->fnhe", q_wide, seen_states, precision=highest)
    denominator = jnp.einsum("fnhd,fhd->fnh", q_wide, seen_sums, precision=highest)
    output = numer / denominator[..., None]
    numer_grad = (grad_wide / denominator[..., None]).astype(jnp.bfloat16)
    denom_grad = -jnp.sum(grad_wide * output, axis=-1) / denominator
    q_grad = jnp.einsum(
        "fnhe,fhde->fnhd", numer_grad.astype(jnp.float32), seen_states, precision=highest
    )
    q_grad = (q_grad + denom_grad[..., None] * seen_sums[:, None]) * slopes(
        queries.reshape(head_shape)
    )
    grad_states = jnp.einsum(
        "fnhd,fnhe->fhde", q_feat, numer_grad, preferred_element_type=jnp.float32
    )
    grad_sums = jnp.einsum("fnhd,fnh->fhd", q_wide, denom_grad, precision=highest)
    grad_states, grad_sums = lax.psum((grad_states, grad_sums), "space")
    later = prefix(
        (jnp.sum(grad_states, axis=0), jnp.sum(grad_sums, axis=0)),
        "tm",
        add_pair,
        (
            jnp.zeros(grad_states.shape[1:], jnp.float32),
            jnp.zeros(grad_sums.shape[1:], jnp.float32),
        ),
        True,
    )
    seen_grads = (
        jnp.einsum("fg,fhde->ghde", visible, grad_states, precision=highest) + later[0][None]
    )
    seen_gsums = jnp.einsum("fg,fhd->ghd", visible, grad_sums, precision=highest) + later[1][None]
    k_grad = jnp.einsum(
        "fnhe,fhde->fnhd", v_heads.astype(jnp.float32), seen_grads, precision=highest
    )
    k_grad = (k_grad + seen_gsums[:, None]) * slopes(keys.reshape(head_shape))
    v_grad = jnp.einsum(
        "fnhd,fhde->fnhe", k_feat.astype(jnp.float32), seen_grads, precision=highest
    )
    out_shape = (frames, rows, cols, width)
    padded = jnp.pad(rimmed.astype(jnp.float32), ((0, 0), (0, 0), (1, 1), (0, 0)))
    input_wide = conv_input.astype(jnp.float32)
    accum = jnp.zeros(conv_grad.shape, jnp.float32)
    kernel_rows = []
    for i in range(3):
        for j in range(3):
            window = padded[:, 2 - i : 2 - i + rows, 2 - j : 2 - j + cols]
            accum = accum + conv_weight[3 * i + j] * window
            kernel_rows.append(jnp.sum(window * input_wide, axis=(0, 1, 2)))
    kernel_total = lax.psum(jnp.stack(kernel_rows), ("tm", "space"))
    tokens_all = frames * rows * cols * lax.axis_size("tm") * lax.axis_size("space")
    kernel_grad = kernel_total * (1.0 / math.sqrt(tokens_all))
    return (
        q_grad.astype(jnp.bfloat16).reshape(out_shape),
        k_grad.astype(jnp.bfloat16).reshape(out_shape),
        v_grad.astype(jnp.bfloat16).reshape(out_shape),
        accum.astype(jnp.bfloat16),
        kernel_grad,
    )


def solution(mesh):
    placed = (
        P("tm", "space", None, None),
        P("tm", "space", None, None),
        P("tm", "space", None, None),
        P("tm", "space", None, None),
        P("tm"),
        P("tm", "space", None, None),
        P("tm", "space", None, None),
        P(),
    )
    return jax.shard_map(
        body,
        mesh=mesh,
        in_specs=placed,
        out_specs=(
            P("tm", "space", None, None),
            P("tm", "space", None, None),
            P("tm", "space", None, None),
            P("tm", "space", None, None),
            P(),
        ),
        check_vma=False,
    )
```

profile of v0, /device:TPU:1, one launch (start us, length us, event | category | flops | bytes accessed | tf_op | source)
XLA Modules:
  0.0 849.6 jit_solution(3635706949680957188)
XLA Ops:
  7.2 2.0 reshape.94
  9.2 2.7 convert_reduce_fusion
  12.8 1.9 fusion.78
  14.8 119.5 %all-reduce.5.cloned.1.call-done = f32[2,20,112,112]{3,2,1,0:T(8,128)} async-done(((f32[2,20,112,112]{3,2,1,0:T(8,128)}), f32[2,20,112,112]{3,2,1,0:T(8,128)}) %all-reduce.5.cloned.1.call-update) | async-done | bytes 2007056 | tf_op jit(solution)/shard_map/psum | solution.py:81
  134.3 2.9 reduce_sum.137
  138.6 2.3 collective-permute-start.1
  140.8 3.3 collective-permute-start
  144.4 2.0 reshape.99
  148.6 44.8 %psum.36 = f32[2,20,112]{2,0,1:T(2,128)S(1)} all-reduce(f32[2,20,112]{2,0,1:T(2,128)S(1)} %copy.57), channel_id=1, replica_groups=mesh['tm'=16,'space'=16] {'space'}, use_global_device_ids=true, to_apply=%region_4.5 | all-reduce | flops 4480 | bytes 35840 | tf_op jit(solution)/shard_map/psum | solution.py:81
  193.5 22.7 %all-gather.4 = f32[16,20,112]{2,1,0:T(8,128)} all-gather(f32[1,20,112]{2,1,0:T(8,128)S(1)} %bitcast.88), channel_id=3, replica_groups=mesh['tm'=16,'space'=16] {'tm'}, dimensions={0}, use_global_device_ids=true | all-gather | bytes 152320 | tf_op jit(solution)/shard_map/all_gather | solution.py:36
  216.2 47.2 %all-gather.9.cloned.1.call-done = f32[320,112,112]{2,1,0:T(8,128)} async-done(((f32[20,112,112]{2,1,0:T(8,128)}), f32[320,112,112]{2,1,0:T(8,128)}) %all-gather.9.cloned.1.call-update) | async-done | bytes 16056336 | tf_op jit(solution)/shard_map/all_gather | solution.py:36
  264.9 3.7 fusion.82
  268.8 1.9 maximum_convert_fusion
  270.7 3.6 fusion.8
  274.5 1.6 stack.39
  276.4 140.1 %all-reduce.7.cloned.1.call-done = f32[2,20,112,112]{3,2,1,0:T(8,128)} async-done(((f32[2,20,112,112]{3,2,1,0:T(8,128)}), f32[2,20,112,112]{3,2,1,0:T(8,128)}) %all-reduce.7.cloned.1.call-update) | async-done | bytes 2007056 | tf_op jit(solution)/shard_map/psum | solution.py:108
  416.5 3.0 reduce_sum.142
  419.5 1.9 select_n.43
  421.4 1.9 select_n.45
  423.9 12.4 %add_convert_fusion = bf16[2,2,32,5632]{3,2,1,0:T(8,128)(2,1)} fusion(f32[2,4,32,5632]{3,2,1,0:T(8,128)} %copy-done, f32[5632]{0:T(1024)S(1)} %get-tuple-element.140, f32[5632]{0:T(1024)S(1)} %get-tuple-element.141, f32[5632]{0:T(1024)S(1)} %get-tuple-element.134, f32[5632]{0:T(1024)S(1)} %get-tuple-element.135, f32[5632]{0:T(1024)S(1)} %get-tuple-element.136, ...), kind=kLoop, calls=%fused_computation.29 | loop fusion | flops 12976128 | bytes 16062464 | tf_op jit(solution)/shard_map/convert_element_type | solution.py:147
  436.3 233.9 %all-reduce.9.cloned.1.call-done = f32[9,5632]{1,0:T(8,128)} async-done(((f32[9,5632]{1,0:T(8,128)}), f32[9,5632]{1,0:T(8,128)}) %all-reduce.9.cloned.1.call-update) | async-done | bytes 202768 | tf_op jit(solution)/shard_map/psum | solution.py:140
  670.2 1.8 broadcast_multiply_fusion
  672.0 6.7 fusion.48
  678.7 1.6 fusion.66
  680.4 2.8 fusion.54
  685.7 44.5 %psum.38 = f32[2,20,112]{2,0,1:T(2,128)S(1)} all-reduce(f32[2,20,112]{2,0,1:T(2,128)S(1)} %bitcast.87), channel_id=1, replica_groups=mesh['tm'=16,'space'=16] {'space'}, use_global_device_ids=true, to_apply=%region_11.12 | all-reduce | flops 4480 | bytes 35840 | tf_op jit(solution)/shard_map/psum | solution.py:108
  730.2 22.3 %all-gather.5 = f32[16,20,112]{2,1,0:T(8,128)} all-gather(f32[1,20,112]{2,1,0:T(8,128)S(1)} %bitcast.89), channel_id=5, replica_groups=mesh['tm'=16,'space'=16] {'tm'}, dimensions={0}, use_global_device_ids=true | all-gather | bytes 152320 | tf_op jit(solution)/shard_map/all_gather | solution.py:36
  752.5 43.3 %all-gather.11.cloned.1.call-done = f32[320,112,112]{2,1,0:T(8,128)} async-done(((f32[20,112,112]{2,1,0:T(8,128)}), f32[320,112,112]{2,1,0:T(8,128)}) %all-gather.11.cloned.1.call-update) | async-done | bytes 16056336 | tf_op jit(solution)/shard_map/all_gather | solution.py:36
  795.9 33.4 %while.27 = (s32[]{:T(128)}, f32[20,112,112]{2,1,0:T(8,128)S(1)}, f32[20,112]{1,0:T(8,128)S(1)}, s32[]{:T(128)}, f32[16,20,112,112]{3,2,1,0:T(8,128)}, /*index=5...) while((s32[]{:T(128)}, f32[20,112,112]{2,1,0:T(8,128)S(1)}, ...), condition=%wide.region_14.15_spmd, body=%wide.region_13.14_spmd.sunk | while | flops 253126 | bytes 3037603 | solution.py:45
  796.0 1.6 bitcast_add_fusion.10
  829.6 5.5 fusion.51
  836.8 2.5 fusion.57
  (128 shorter events, 47.1 us)
Async XLA Ops:
  7.2 127.1 %all-reduce.5.cloned.1.call-start = ((), (), s32[]{:S(2)}) async-start(), calls=%async_computation | async-start | bytes 4587520 | tf_op jit(solution)/shard_map/psum | solution.py:81
  9.2 5.5 copy-start.4
  12.8 1.9 copy-start.6
  14.8 122.6 %copy-start.3 = (bf16[2,2,32,5632]{3,2,1,0:T(8,128)(2,1)S(1)}, bf16[2,2,32,5632]{3,2,1,0:T(8,128)(2,1)}, u32[]{:S(2)}) copy-start(bf16[2,2,32,5632]{3,2,1,0:T(8,128)(2,1)} %param.18) | copy-start | bytes 4325380
  14.8 248.6 %all-gather.9.cloned.1.call-start = ((), (), s32[]{:S(2)}) async-start(), calls=%async_computation.3 | async-start | bytes 19496960 | tf_op jit(solution)/shard_map/all_gather | solution.py:36
  137.2 7.0 copy-start.22
  137.2 7.2 copy-start.17
  137.3 9.2 %copy-start.18 = (bf16[2,2,32,2240]{3,2,1,0:T(8,128)(2,1)S(1)}, bf16[2,2,32,2240]{3,2,1,0:T(8,128)(2,1)}, u32[]{:S(2)}) copy-start(bf16[2,2,32,2240]{3,2,1,0:T(8,128)(2,1)} %param.12) | copy-start | bytes 1720324
  137.3 279.2 %all-reduce.7.cloned.1.call-start = ((), (), s32[]{:S(2)}) async-start(), calls=%async_computation.1 | async-start | bytes 4587520 | tf_op jit(solution)/shard_map/psum | solution.py:108
  138.6 130.2 %collective-permute-start.1 = (bf16[2,1,32,5632]{3,2,1,0:T(8,128)(2,1)}, bf16[2,1,32,5632]{3,2,1,0:T(8,128)(2,1)}, u32[]{:S(2)}, u32[]{:S(2)}) collective-permute-start(bf16[2,1,32,5632]{3,2,1,0:T(8,128)(2,1)} %get-tuple-element.169), channel_id=1, source_target_pairs={{1,0},{2,1},{3,2},{4,3},{5,4},{6,5},{7,6},{8,7},{9,8},{10,9},{11,1... | collective-permute-start | bytes 2162696 | tf_op jit(solution)/shard_map/ppermute | solution.py:25
  140.8 127.9 %collective-permute-start = (bf16[2,1,32,5632]{3,2,1,0:T(8,128)(2,1)}, bf16[2,1,32,5632]{3,2,1,0:T(8,128)(2,1)}, u32[]{:S(2)}, u32[]{:S(2)}) collective-permute-start(bf16[2,1,32,5632]{3,2,1,0:T(8,128)(2,1)} %get-tuple-element.168), channel_id=1, source_target_pairs={{0,1},{1,2},{2,3},{3,4},{4,5},{5,6},{6,7},{7,8},{8,9},{9,10},{10,1... | collective-permute-start | bytes 2162696 | tf_op jit(solution)/shard_map/ppermute | solution.py:23
  148.6 116.3 %copy-start.14 = (bf16[2,64,20,112]{3,2,1,0:T(8,128)(2,1)}, bf16[2,64,20,112]{3,2,1,0:T(8,128)(2,1)S(1)}, u32[]{:S(2)}) copy-start(bf16[2,64,20,112]{3,2,1,0:T(8,128)(2,1)S(1)} %reshape.95) | copy-start | bytes 1720324
  263.8 4.8 copy-start.20
  268.7 401.5 %all-reduce.9.cloned.1.call-start = ((), (), s32[]{:S(2)}) async-start(), calls=%async_computation.2 | async-start | bytes 720896 | tf_op jit(solution)/shard_map/psum | solution.py:140
  268.7 1.9 copy-start.13
  270.6 3.6 copy-start
  276.2 143.3 %copy-start.9 = (f32[2,2,32,2240]{3,2,1,0:T(8,128)S(1)}, f32[2,2,32,2240]{3,2,1,0:T(8,128)}, u32[]{:S(2)}) copy-start(f32[2,2,32,2240]{3,2,1,0:T(8,128)} %get-tuple-element.172) | copy-start | bytes 3440644
  276.2 519.6 %all-gather.11.cloned.1.call-start = ((), (), s32[]{:S(2)}) async-start(), calls=%async_computation.4 | async-start | bytes 19496960 | tf_op jit(solution)/shard_map/all_gather | solution.py:36
  419.5 1.9 copy-start.10
  421.4 1.9 copy-start.19
  423.8 248.1 %copy-start.21 = (f32[2,20,112]{2,0,1:T(2,128)S(1)}, f32[2,20,112]{2,0,1:T(2,128)}, u32[]{:S(2)}) copy-start(f32[2,20,112]{2,0,1:T(2,128)} %copy-done.20) | copy-start | bytes 53764
  423.8 248.1 %copy-start.1 = (f32[2,20,112,112]{3,2,1,0:T(8,128)S(1)}, f32[2,20,112,112]{3,2,1,0:T(8,128)}, u32[]{:S(2)}) copy-start(f32[2,20,112,112]{3,2,1,0:T(8,128)} %all-reduce.5.cloned.1.call-done) | copy-start | bytes 6021124
  671.9 6.7 copy-start.11
  671.9 6.7 copy-start.15
  678.7 1.7 copy-start.12
  683.1 1.9 copy-start.16
  795.9 33.7 %copy-start.2 = (f32[2,20,112,112]{3,2,1,0:T(8,128)S(1)}, f32[2,20,112,112]{3,2,1,0:T(8,128)}, u32[]{:S(2)}) copy-start(f32[2,20,112,112]{3,2,1,0:T(8,128)} %all-reduce.7.cloned.1.call-done) | copy-start | bytes 6021124
  829.6 5.6 copy-start.7
  835.2 1.3 copy-start.5
  835.2 1.6 copy-start.8
Sparse Core Ops, SparseCore 0:
  14.9 119.3 all-reduce.4
  137.4 125.9 all-gather.8
  268.8 147.6 all-reduce.6
  422.5 247.6 all-reduce.8
  672.5 123.2 all-gather.10
where the time goes:
time: 851 us; the launch traced here: 850 us
  waiting for transfers between devices  584 us (69%)
  blocking collectives  134 us (16%)
  other arithmetic  63.2 us (7%)
  matrix products  28.2 us (3%)
  local copies, waits for them, and re-layouts  19.3 us (2%)
  between operations  14.3 us (2%)
    psum x1, waiting for transfers between devices, body(): kernel_total = lax.psum(jnp.stack(kernel_rows), ('tm', 'space'))  234 us
    psum x1, waiting for transfers between devices, body(): grad_states, grad_sums = lax.psum((grad_states, grad_sums), 'space')  140 us
    psum x1, waiting for transfers between devices, body(): states, sums = lax.psum((states, sums), 'space')  119 us
    all_gather x2, waiting for transfers between devices, prefix(): gathered = jax.tree.map(lambda a: lax.all_gather(a, axis), part)  90.5 us
    all_gather x2, blocking collectives, prefix(): gathered = jax.tree.map(lambda a: lax.all_gather(a, axis), part)  45 us
    psum x1, blocking collectives, body(): states, sums = lax.psum((states, sums), 'space')  44.8 us
    psum x1, blocking collectives, body(): grad_states, grad_sums = lax.psum((grad_states, grad_sums), 'space')  44.5 us
    add x30, other arithmetic, add_pair(): return (earlier[0] + later[0], earlier[1] + later[1])  33.3 us
  transfers between devices with their start and end apart: 7, of which 5 were waited for; matrix products, arithmetic and copies ran while one was open for 6% of the time, Pallas kernels for 0%

commit v1 on v0

v1 whole, which is shorter than its diff:
```python
import functools
import math

import jax
import jax.numpy as jnp
from jax import lax
from jax.experimental import pallas as pl
from jax.experimental.pallas import tpu as pltpu
from jax.sharding import PartitionSpec as P

HEADS = 20
HD = 112
LANES = 128
F32 = jnp.float32
BF16 = jnp.bfloat16
MESH = pl.DeviceIdType.MESH

CHUNK_HEADS = 10
NCH = 2
NZ = 8
NR = 4
ROWS = 144
HALF = 80
CROWS = NZ * ROWS
KROWS = 96
KTOT = NZ * KROWS
TOKENS = 128
HALFTOK = 64
GROUP = 5


def lifted(wide):
    return jnp.where(wide > 0, wide + 1.0, jnp.exp(jnp.minimum(wide, 0.0)))


def dot(a, b, ca, cb):
    return lax.dot_general(a, b, (((ca,), (cb,)), ((), ())), preferred_element_type=F32)


ORDER = (4, 3, 5, 2, 6, 1, 7)


class Place:
    def __init__(self):
        t = lax.axis_index("tm")
        s = lax.axis_index("space")
        self.t, self.s = t, s
        self.core = lax.rem(s, 2)
        self.z = lax.div(s, 2)
        self.x = lax.div(t, NR)
        self.y = lax.rem(t, NR)
        self.sibling = (t, s + 1 - 2 * self.core)
        self.up = (t, lax.rem(s + 2, 2 * NZ))
        self.down = (t, lax.rem(s + 2 * NZ - 2, 2 * NZ))
        self.ys = [(self.x * NR + lax.rem(self.y + k, NR), s) for k in (1, 2, 3)]
        self.xs = [(lax.rem(self.x + k, NR) * NR + self.y, s) for k in (1, 2, 3)]
        self.cross = (t, lax.rem(s + 2 * NZ - 1 + 2 * self.core, 2 * NZ))
        self.prev = (t, lax.rem(s + 2 * NZ - 1, 2 * NZ))
        self.next = (t, lax.rem(s + 1, 2 * NZ))


def low_lane(wide):
    return lax.broadcasted_iota(jnp.int32, wide.shape, 1) == HD + 1


def pack(wide):
    rounded = wide.astype(BF16).astype(F32)
    rest = pltpu.roll(wide - rounded, 1, 1)
    return jnp.where(low_lane(wide), wide + rest, rounded).astype(BF16)


def spread(wide):
    lane = lax.broadcasted_iota(jnp.int32, wide.shape, 1)
    return jnp.where((lane == HD + 1) | (lane == HD + 2), pltpu.roll(wide, 1, 1), wide)


class Sum:
    def __init__(self, at, core, bufs, rows):
        self.at, self.core, self.rows = at, core, rows
        self.pending = []
        for name, ref in bufs.items():
            setattr(self, name, ref)

    def sl(self, o, lo=0, n=None):
        n = self.rows if n is None else n
        return pl.ds(pl.multiple_of(o * self.rows + lo, 16), n)

    def remote(self, src, dst, ss, rr, dev):
        return pltpu.make_async_remote_copy(
            src_ref=src, dst_ref=dst, send_sem=ss, recv_sem=rr, device_id=dev, device_id_type=MESH
        )

    def exchange_copy(self):
        return self.remote(self.loc, self.xbuf, self.ex_s, self.ex_r, self.at.sibling)

    def go(self, make):
        make().start()
        self.pending.append(make)

    def drain(self):
        for make in self.pending:
            make().wait_send()

    def forward_copy(self, j):
        ref = self.forwarded(j)
        return self.remote(ref, ref, self.fw_s.at[j], self.fw_r.at[j], self.at.sibling)

    def finish(self):
        for j in range(self.forwards):
            self.forward_copy(j).wait_recv()


class Direct(Sum):
    forwards = NZ

    def __init__(self, at, core, bufs, rows, mode):
        super().__init__(at, core, bufs, rows)
        self.mode = mode

    def away(self, j):
        return lax.rem(self.at.z + j, NZ)

    def peer(self, j):
        return (self.at.t, lax.rem(self.at.s + 2 * j, 2 * NZ))

    def round(self, wide):
        return wide.astype(BF16) if self.mode == "sum" else pack(wide)

    def scatter_copy(self, j):
        return self.remote(
            self.send.at[self.sl(self.away(j))], self.recv.at[j - 1], self.rs_s.at[j - 1], self.rs_r.at[j - 1], self.peer(j)
        )

    def scatter(self):
        self.exchange_copy().wait_recv()
        self.send[...] = self.round(self.mine[...] + self.xbuf[...])
        for j in ORDER:
            self.go(functools.partial(self.scatter_copy, j))

    def tm_copy(self, axis, k):
        if axis == "y":
            return self.remote(self.ysend, self.yrecv.at[k], self.y_s.at[k], self.y_r.at[k], self.at.ys[k])
        return self.remote(self.xsend, self.xrecv.at[k], self.x_s.at[k], self.x_r.at[k], self.at.xs[k])

    def weight(self, place, k):
        if self.mode == "sum":
            return 1.0
        before = (place - (k + 1) >= 0).astype(F32)
        return before if self.mode == "prefix" else 1.0 - before

    def close(self):
        own = self.mine[self.sl(self.at.z)] + self.xbuf[self.sl(self.at.z)]
        for j in ORDER[::-1]:
            self.scatter_copy(j).wait_recv()
            own = own + self.recv[j - 1].astype(F32)
        self.own[...] = own
        self.ysend[...] = self.round(own)
        for k in (1, 0, 2):
            self.go(functools.partial(self.tm_copy, "y", k))

    def over_y(self):
        total = self.own[...]
        part = total
        for k in (0, 2, 1):
            self.tm_copy("y", k).wait_recv()
            got = self.yrecv[k].astype(F32)
            total = total + got
            part = part + self.weight(self.at.y, k) * got
        self.own[...] = part
        self.xsend[...] = self.round(total)
        for k in (1, 0, 2):
            self.go(functools.partial(self.tm_copy, "x", k))

    def over_x(self):
        part = self.own[...]
        for k in (0, 2, 1):
            self.tm_copy("x", k).wait_recv()
            part = part + self.weight(self.at.x, k) * self.xrecv[k].astype(F32)
        self.gbuf[self.sl(self.at.z)] = self.round(part)
        for j in ORDER:
            self.go(functools.partial(self.gather_copy, j))
        self.go(functools.partial(self.forward_copy, 0))

    def gather_copy(self, j):
        ref = self.gbuf.at[self.sl(self.at.z)]
        return self.remote(ref, ref, self.ag_s.at[j - 1], self.ag_r.at[j - 1], self.peer(j))

    def arrived_copy(self, j):
        ref = self.gbuf.at[self.sl(self.away(NZ - j))]
        return self.remote(ref, ref, self.ag_s.at[j - 1], self.ag_r.at[j - 1], self.peer(j))

    def forwarded(self, j):
        return self.gbuf.at[self.sl(self.away(NZ - j) if j else self.at.z)]

    def gather(self):
        for j in ORDER[::-1]:
            self.arrived_copy(j).wait_recv()
            self.go(functools.partial(self.forward_copy, j))


class Ring(Sum):
    forwards = 9

    def part(self, d, far):
        if not far:
            return 0, self.rows
        return (0, HALF) if d == 0 else (HALF, self.rows - HALF)

    def dev(self, d):
        return self.at.up if d == 0 else self.at.down

    def take(self):
        self.exchange_copy().wait_recv()
        self.acc[...] = self.mine[...] + self.xbuf[...]

    def scatter_copy(self, d, s):
        part = pl.ds(*self.part(d, s == 0))
        return self.remote(
            self.send.at[d, s, part], self.recv.at[d, s, part], self.rs_s.at[d, s], self.rs_r.at[d, s], self.dev(d)
        )

    def scatter(self, s):
        for d in (0, 1):
            o = lax.rem(self.at.z + (4 - s if d == 0 else 4 + s), NZ)
            lo, n = self.part(d, True)
            olo, on = self.part(1 - d, True)
            if s > 0:
                self.scatter_copy(d, s - 1).wait_recv()
            if s < 2:
                wide = self.acc[self.sl(o, lo, n)]
                if s == 1:
                    wide = wide + self.recv[d, 0, pl.ds(lo, n)].astype(F32)
                    self.send[d, 1, pl.ds(olo, on)] = pack(self.acc[self.sl(o, olo, on)])
                self.send[d, s, pl.ds(lo, n)] = pack(wide)
            else:
                self.send[d, s] = pack(self.acc[self.sl(o)] + self.recv[d, s - 1].astype(F32))
            self.go(functools.partial(self.scatter_copy, d, s))

    def close(self):
        self.scatter_copy(0, 3).wait_recv()
        self.scatter_copy(1, 3).wait_recv()
        own = self.acc[self.sl(self.at.z)] + self.recv[0, 3].astype(F32) + self.recv[1, 3].astype(F32)
        self.gbuf[self.sl(self.at.z)] = pack(own)

    def slice_from(self, d, s, far):
        o = lax.rem(self.at.z + (NZ - s if d == 0 else s), NZ)
        return self.gbuf.at[self.sl(o, *self.part(d, far))]

    def gather_copy(self, d, s):
        ref = self.slice_from(d, s, s == 3)
        return self.remote(ref, ref, self.ag_s.at[d, s], self.ag_r.at[d, s], self.dev(d))

    def arrived_copy(self, d, s):
        ref = self.slice_from(d, s + 1, s == 3)
        return self.remote(ref, ref, self.ag_s.at[d, s], self.ag_r.at[d, s], self.dev(d))

    def forwarded(self, j):
        s, d = (j + 1) // 2, (j + 1) % 2
        return self.slice_from(d, s, s == 4)

    def gather(self, s):
        if s > 0:
            for d in (0, 1):
                self.arrived_copy(d, s - 1).wait_recv()
        if s < 4:
            for d in (0, 1):
                self.go(functools.partial(self.gather_copy, d, s))
        for j in [0] if s == 0 else [2 * s - 1, 2 * s]:
            self.go(functools.partial(self.forward_copy, j))


def kernel(scale, *refs):
    (
        q_hbm, k_hbm, v_hbm, g_hbm, bs_ref, ci_hbm, cg_hbm, w_hbm,
        qo_hbm, ko_hbm, vo_hbm, io_hbm, wo_hbm,
        q_in, k_in, v_in, g_in, ci_in, cg_in, w_in,
        qo, ko, vo, io, wo,
        qp, kp, vp, gp, halo, ktaps,
        loc, xbuf, gbuf,
        dsend, drecv, down, dysend, dyrecv, dxsend, dxrecv,
        racc, rsend, rrecv,
        kloc, kxbuf, kgbuf, ksend, krecv, kown, kysend, kyrecv, kxsend, kxrecv,
        in_sem, out_sem, halo_s, halo_r,
        ex_s, ex_r, drs_s, drs_r, dag_s, dag_r, y_s, y_r, x_s, x_r,
        rrs_s, rrs_r, rag_s, rag_r, fw_s, fw_r,
    ) = refs
    at = Place()
    first_core, second_core = at.core == 0, at.core == 1
    channels = io.shape[-1]
    tiles = channels // LANES

    barrier = pltpu.get_barrier_semaphore()
    others = [at.sibling, at.cross, *at.ys, *at.xs]
    others += [(at.t, lax.rem(at.s + 2 * j, 2 * NZ)) for j in range(1, NZ)]
    for dev in others:
        pl.semaphore_signal(barrier, inc=1, device_id=dev, device_id_type=MESH)

    loads = [
        pltpu.make_async_copy(src, dst, in_sem.at[i])
        for i, (src, dst) in enumerate(
            [(k_hbm, k_in), (v_hbm, v_in), (q_hbm, q_in), (g_hbm, g_in), (cg_hbm, cg_in), (ci_hbm, ci_in), (w_hbm, w_in)]
        )
    ]
    for load in loads:
        load.start()

    def direct(i):
        return Direct(
            at, 0,
            dict(
                loc=loc.at[i, 1], mine=loc.at[i, 0], xbuf=xbuf.at[i], gbuf=gbuf.at[i, 0], send=dsend.at[i], recv=drecv.at[i],
                own=down.at[i], ysend=dysend.at[i], yrecv=dyrecv.at[i], xsend=dxsend.at[i], xrecv=dxrecv.at[i],
                ex_s=ex_s.at[i], ex_r=ex_r.at[i], rs_s=drs_s.at[i], rs_r=drs_r.at[i], ag_s=dag_s.at[i], ag_r=dag_r.at[i],
                y_s=y_s.at[i], y_r=y_r.at[i], x_s=x_s.at[i], x_r=x_r.at[i], fw_s=fw_s.at[i], fw_r=fw_r.at[i],
            ),
            ROWS, "prefix" if i < NCH else "suffix",
        )

    def ring(i):
        return Ring(
            at, 1,
            dict(
                loc=loc.at[i, 0], mine=loc.at[i, 1], xbuf=xbuf.at[i], gbuf=gbuf.at[i, 1], acc=racc.at[i],
                send=rsend.at[i], recv=rrecv.at[i],
                ex_s=ex_s.at[i], ex_r=ex_r.at[i], rs_s=rrs_s.at[i], rs_r=rrs_r.at[i], ag_s=rag_s.at[i], ag_r=rag_r.at[i],
                fw_s=fw_s.at[i], fw_r=fw_r.at[i],
            ),
            ROWS,
        )

    directs = [direct(i) for i in range(2 * NCH)]
    rings = [ring(i) for i in range(2 * NCH)]
    i = 2 * NCH
    ksum = Direct(
        at, 1,
        dict(
            loc=kloc, mine=kloc, xbuf=kxbuf, gbuf=kgbuf, send=ksend, recv=krecv,
            own=kown, ysend=kysend, yrecv=kyrecv, xsend=kxsend, xrecv=kxrecv,
            ex_s=ex_s.at[i], ex_r=ex_r.at[i], rs_s=drs_s.at[i], rs_r=drs_r.at[i], ag_s=dag_s.at[i], ag_r=dag_r.at[i],
            y_s=y_s.at[i], y_r=y_r.at[i], x_s=x_s.at[i], x_r=x_r.at[i], fw_s=fw_s.at[i], fw_r=fw_r.at[i],
        ),
        KROWS, "sum",
    )

    lane = lax.broadcasted_iota(jnp.int32, (TOKENS, LANES), 1)
    ones = ((lane == HD) | (lane == HD + 1)).astype(F32).astype(BF16)
    zero = jnp.zeros((TOKENS, LANES), BF16)

    def prepare(src, dst, heads, fill, lift):
        for h in heads:
            part = src[:, h * HD : (h + 1) * HD]
            if lift:
                part = lifted(part.astype(F32)).astype(BF16)
            dst[h] = fill
            dst[h, :, 0:HD] = part

    for i in range(2 * NCH):
        for j in range(2):
            loc[i, j, CHUNK_HEADS * HD :, :] = jnp.zeros((CROWS - CHUNK_HEADS * HD, LANES), F32)
    kloc[tiles * 16 :, :] = jnp.zeros((KTOT - tiles * 16, LANES), F32)

    @pl.when(at.s == 0)
    def _():
        halo[0] = jnp.zeros(halo.shape[1:], BF16)

    @pl.when(at.s == 2 * NZ - 1)
    def _():
        halo[1] = jnp.zeros(halo.shape[1:], BF16)

    pl.semaphore_wait(barrier, len(others))

    def halo_copy(d, f):
        return pltpu.make_async_remote_copy(
            src_ref=cg_hbm.at[f, 1 - d],
            dst_ref=halo.at[d, f],
            send_sem=halo_s.at[d, f],
            recv_sem=halo_r.at[d, f],
            device_id=at.next if d == 0 else at.prev,
            device_id_type=MESH,
        )

    has_next, has_prev = at.s < 2 * NZ - 1, at.s > 0

    def halo_start(f):
        @pl.when(has_next)
        def _():
            halo_copy(0, f).start()

        @pl.when(has_prev)
        def _():
            halo_copy(1, f).start()

    def halo_wait(f):
        @pl.when(has_prev)
        def _():
            halo_copy(0, f).wait_recv()

        @pl.when(has_next)
        def _():
            halo_copy(1, f).wait_recv()

    halo_start(0)
    loads[0].wait()
    loads[1].wait()

    def head_rows(h, n):
        return pl.ds(pl.multiple_of(h * HD, 16), n)

    def exchange(i):
        @pl.when(first_core)
        def _():
            directs[i].exchange_copy().start()

        @pl.when(second_core)
        def _():
            rings[i].exchange_copy().start()

    def states(c):
        no_low = lane[:HD] != HD + 1

        def some(n, _):
            heads = [n * GROUP + u for u in range(GROUP)]
            ks = [kp[c * CHUNK_HEADS + h] for h in heads]
            vs = [vp[c * CHUNK_HEADS + h] for h in heads]
            both = [dot(k, v, 0, 0)[:HD] for k, v in zip(ks, vs)]
            lone = [dot(k[HALFTOK:], v[HALFTOK:], 0, 0)[:HD] for k, v in zip(ks, vs)]
            for h, b, l in zip(heads, both, lone):
                loc[c, 0, head_rows(h, HD)] = jnp.where(no_low, b, 0.0)
                loc[c, 1, head_rows(h, HD)] = jnp.where(no_low, l, 0.0)
            return 0

        lax.fori_loop(0, CHUNK_HEADS // GROUP, some, 0)
        exchange(c)

    chunk = [range(c * CHUNK_HEADS, (c + 1) * CHUNK_HEADS) for c in range(NCH)]
    for c in range(NCH):
        prepare(k_in, kp, chunk[c], zero, True)
        prepare(v_in, vp, chunk[c], ones, False)
        states(c)

    col = lax.broadcasted_iota(jnp.int32, (32, LANES), 0)
    not_first, not_last = col > 0, col < 31

    def conv_tile(f, n, _):
        at_lane = pl.ds(pl.multiple_of(n * LANES, LANES), LANES)
        taps = [w_in[t : t + 1, at_lane] for t in range(9)]
        sums9 = [None] * 9
        rows = [halo[0, f, :, at_lane], cg_in[f, 0, :, at_lane], cg_in[f, 1, :, at_lane], halo[1, f, :, at_lane]]
        outs = [None, None]
        inner = [ci_in[f, r, :, at_lane].astype(F32) for r in range(2)]
        for m in range(4):
            wide = rows[m].astype(F32)
            later = jnp.where(not_last, pltpu.roll(wide, 31, 0), 0.0)
            earlier = jnp.where(not_first, pltpu.roll(wide, 1, 0), 0.0)
            for r in range(2):
                i = r + 2 - m
                if 0 <= i <= 2:
                    for j, window in enumerate((later, wide, earlier)):
                        t = 3 * i + j
                        add = taps[t] * window
                        outs[r] = add if outs[r] is None else outs[r] + add
                        prod = window * inner[r]
                        prod = prod[0:8] + prod[8:16] + (prod[16:24] + prod[24:32])
                        sums9[t] = prod if sums9[t] is None else sums9[t] + prod
        for r in range(2):
            io[f, r, :, at_lane] = outs[r].astype(BF16)
        total = jnp.concatenate(
            [jnp.sum(a, axis=0, keepdims=True) for a in sums9] + [jnp.zeros((7, LANES), F32)], axis=0
        )
        place = pl.ds(pl.multiple_of(n * 16, 16), 16)
        if f == 0:
            ktaps[place] = total
        else:
            kloc[place] = ktaps[place] + total
        return 0

    def conv(f, a, b):
        lax.fori_loop(a, b, functools.partial(conv_tile, f), 0)

    def conv_done():
        pltpu.make_async_copy(io, io_hbm, out_sem.at[3]).start()

        @pl.when(first_core)
        def _():
            ksum.exchange_copy().start()

    bs = bs_ref[1].astype(F32)

    def queries(c):
        lanes = lane[:HALFTOK]

        def some(n, _):
            heads = [n * GROUP + u for u in range(GROUP)]
            whole = [(qp[c * CHUNK_HEADS + h], gp[c * CHUNK_HEADS + h]) for h in heads]
            states = []
            for h in heads:
                last = gbuf[c, 0, head_rows(h, LANES)].astype(F32)
                lone = gbuf[c, 1, head_rows(h, LANES)].astype(F32)
                first = pack(last - bs * lone).astype(F32)
                states.append((spread(first).astype(BF16), spread(last).astype(BF16)))
            parts = [
                (q[f * HALFTOK : (f + 1) * HALFTOK], g[f * HALFTOK : (f + 1) * HALFTOK].astype(F32), s[f])
                for (q, g), s in zip(whole, states)
                for f in range(2)
            ]
            numers = [dot(q, s, 1, 0) for q, _, s in parts]
            dns = []
            for (_, g, _), numer in zip(parts, numers):
                inv = 1.0 / (numer[:, HD : HD + 1] + numer[:, HD + 2 : HD + 3])
                dd = -(jnp.sum(g * numer, axis=1, keepdims=True) * inv) * inv
                hi = dd.astype(BF16).astype(F32)
                wide = jnp.where((lanes == HD) | (lanes == HD + 2), hi, g * inv)
                dns.append(jnp.where(lanes == HD + 1, dd - hi, wide).astype(BF16))
            grads = [
                (dot(dn, s, 1, 1) * jnp.minimum(q.astype(F32), 1.0)).astype(BF16) for (q, _, s), dn in zip(parts, dns)
            ]
            both = [
                dot(q, jnp.concatenate(dns[2 * u : 2 * u + 2], axis=0), 0, 0)[:HD] for u, (q, _) in enumerate(whole)
            ]
            lone = [dot(parts[2 * u][0], dns[2 * u], 0, 0)[:HD] for u in range(GROUP)]
            for u, h in enumerate(heads):
                loc[NCH + c, 0, head_rows(h, HD)] = both[u]
                loc[NCH + c, 1, head_rows(h, HD)] = lone[u]
                gp[c * CHUNK_HEADS + h] = jnp.concatenate(grads[2 * u : 2 * u + 2], axis=0)
            return 0

        lax.fori_loop(0, CHUNK_HEADS // GROUP, some, 0)
        exchange(NCH + c)

    def keys(c):
        def some(n, _):
            heads = [n * GROUP + u for u in range(GROUP)]
            whole = [(kp[c * CHUNK_HEADS + h], vp[c * CHUNK_HEADS + h]) for h in heads]
            states = []
            for h in heads:
                first = gbuf[NCH + c, 0, head_rows(h, LANES)]
                lone = gbuf[NCH + c, 1, head_rows(h, LANES)]
                states.append((first, pack(first.astype(F32) - bs * lone.astype(F32))))
            outs = []
            for (k, v), s in zip(whole, states):
                kg = jnp.concatenate(
                    [dot(v[f * HALFTOK : (f + 1) * HALFTOK], s[f], 1, 1) for f in range(2)], axis=0
                )
                vg = jnp.concatenate(
                    [dot(k[f * HALFTOK : (f + 1) * HALFTOK], s[f], 1, 0) for f in range(2)], axis=0
                )
                outs.append(((kg * jnp.minimum(k.astype(F32), 1.0)).astype(BF16), vg.astype(BF16)))
            for h, (kg, vg) in zip(heads, outs):
                kp[c * CHUNK_HEADS + h] = kg
                vp[c * CHUNK_HEADS + h] = vg
            return 0

        lax.fori_loop(0, CHUNK_HEADS // GROUP, some, 0)

    def write(src, dst, heads):
        for h in heads:
            dst[:, h * HD : (h + 1) * HD] = src[h, :, 0:HD]

    def prepare_queries():
        loads[2].wait()
        loads[3].wait()
        for c in range(NCH):
            prepare(q_in, qp, chunk[c], zero, True)
            prepare(g_in, gp, chunk[c], zero, False)

    def conv_loads():
        for n in (4, 5, 6):
            loads[n].wait()

    half = tiles // 2

    @pl.when(first_core)
    def _():
        a, b = directs[0], directs[1]
        a.scatter()
        b.scatter()
        prepare_queries()
        a.close()
        b.close()
        halo_start(1)
        conv_loads()
        halo_wait(0)
        conv(0, 0, half)
        a.over_y()
        b.over_y()
        conv(0, half, tiles)
        a.over_x()
        b.over_x()
        halo_wait(1)
        conv(1, 0, half)
        a.gather()
        b.gather()

    @pl.when(second_core)
    def _():
        a, b = rings[0], rings[1]
        a.take()
        b.take()
        prepare_queries()
        for s in range(4):
            a.scatter(s)
            b.scatter(s)
        halo_start(1)
        a.close()
        b.close()
        for s in range(5):
            if s == 1:
                conv_loads()
                halo_wait(0)
            if s >= 1:
                conv(0, tiles * (s - 1) // 4, tiles * s // 4)
            a.gather(s)
            b.gather(s)
        halo_wait(1)
        conv(1, 0, half)

    def finish(i):
        @pl.when(first_core)
        def _():
            rings[i].finish()

        @pl.when(second_core)
        def _():
            directs[i].finish()

    for c in range(NCH):
        finish(c)
        queries(c)

    @pl.when(first_core)
    def _():
        a, b = directs[NCH], directs[NCH + 1]
        a.scatter()
        b.scatter()
        conv(1, half, tiles)
        conv_done()
        a.close()
        b.close()
        write(gp, qo, chunk[0])
        a.over_y()
        b.over_y()
        write(gp, qo, chunk[1])
        pltpu.make_async_copy(qo, qo_hbm, out_sem.at[0]).start()
        a.over_x()
        b.over_x()
        a.gather()
        b.gather()

    @pl.when(second_core)
    def _():
        a, b = rings[NCH], rings[NCH + 1]
        a.take()
        b.take()
        conv(1, half, tiles)
        conv_done()
        ksum.scatter()
        for s in range(4):
            a.scatter(s)
            b.scatter(s)
        ksum.close()
        a.close()
        b.close()
        for s in range(5):
            a.gather(s)
            b.gather(s)
            if s == 0:
                ksum.over_y()
                write(gp, qo, chunk[0])
            if s == 1:
                ksum.over_x()
                write(gp, qo, chunk[1])
                pltpu.make_async_copy(qo, qo_hbm, out_sem.at[0]).start()
        ksum.gather()

    for c in range(NCH):
        finish(NCH + c)
        keys(c)
        write(kp, ko, chunk[c])
        write(vp, vo, chunk[c])
    pltpu.make_async_copy(ko, ko_hbm, out_sem.at[1]).start()
    pltpu.make_async_copy(vo, vo_hbm, out_sem.at[2]).start()

    @pl.when(first_core)
    def _():
        ksum.finish()

    for n in range(tiles):
        wo[:, n * LANES : (n + 1) * LANES] = kgbuf[n * 16 : n * 16 + 16].astype(F32)[:9] * scale
    pltpu.make_async_copy(wo, wo_hbm, out_sem.at[4]).start()

    @pl.when(first_core)
    def _():
        for s in directs:
            s.exchange_copy().wait_send()
            s.drain()
        ksum.exchange_copy().wait_send()

    @pl.when(second_core)
    def _():
        for s in rings:
            s.exchange_copy().wait_send()
            s.drain()
        ksum.drain()

    for f in range(2):

        @pl.when(has_next)
        def _():
            halo_copy(0, f).wait_send()

        @pl.when(has_prev)
        def _():
            halo_copy(1, f).wait_send()

    for i, (src, dst) in enumerate([(qo, qo_hbm), (ko, ko_hbm), (vo, vo_hbm), (io, io_hbm), (wo, wo_hbm)]):
        pltpu.make_async_copy(src, dst, out_sem.at[i]).wait()


def move(*refs):
    srcs, dsts, bufs, in_sem, out_sem = refs[:5], refs[5:10], refs[10:15], refs[15], refs[16]
    loads = [pltpu.make_async_copy(s, b, in_sem.at[i]) for i, (s, b) in enumerate(zip(srcs, bufs))]
    stores = [pltpu.make_async_copy(b, d, out_sem.at[i]) for i, (b, d) in enumerate(zip(bufs, dsts))]
    for load in loads:
        load.start()
    for load, store in zip(loads, stores):
        load.wait()
        store.start()
    for store in stores:
        store.wait()


def body(queries, keys, values, out_grad, block_start, conv_input, conv_grad, conv_weight):
    frames, rows, cols, width = queries.shape
    channels = conv_grad.shape[-1]
    tokens = frames * rows * cols
    all_tokens = tokens * lax.axis_size("tm") * lax.axis_size("space")
    flat = (tokens, width)
    conv_shape = conv_grad.shape
    n = 2 * NCH
    vm, dma = pltpu.VMEM, pltpu.SemaphoreType.DMA

    def tm_bufs(lead, rows_):
        return [
            vm((*lead, rows_, LANES), F32),
            vm((*lead, rows_, LANES), BF16),
            vm((*lead, 3, rows_, LANES), BF16),
            vm((*lead, rows_, LANES), BF16),
            vm((*lead, 3, rows_, LANES), BF16),
        ]

    shapes = (
        jax.ShapeDtypeStruct(flat, BF16),
        jax.ShapeDtypeStruct(flat, BF16),
        jax.ShapeDtypeStruct(flat, BF16),
        jax.ShapeDtypeStruct(conv_shape, BF16),
        jax.ShapeDtypeStruct(conv_weight.shape, F32),
    )
    outs = pl.pallas_call(
        functools.partial(kernel, 1.0 / math.sqrt(all_tokens)),
        out_shape=shapes,
        in_specs=[pl.BlockSpec(memory_space=pl.ANY)] * 4
        + [pl.BlockSpec(memory_space=pltpu.SMEM)]
        + [pl.BlockSpec(memory_space=pl.ANY)] * 3,
        out_specs=[pl.BlockSpec(memory_space=pl.ANY)] * 5,
        scratch_shapes=[
            *[vm(flat, BF16)] * 4,
            vm(conv_shape, BF16),
            vm(conv_shape, BF16),
            vm(conv_weight.shape, F32),
            *[vm(flat, BF16)] * 3,
            vm(conv_shape, BF16),
            vm(conv_weight.shape, F32),
            *[vm((HEADS, tokens, LANES), BF16)] * 4,
            vm((2, frames, cols, channels), BF16),
            vm((KTOT, LANES), F32),
            vm((n, 2, CROWS, LANES), F32),
            vm((n, CROWS, LANES), F32),
            vm((n, 2, CROWS, LANES), BF16),
            vm((n, CROWS, LANES), BF16),
            vm((n, NZ - 1, ROWS, LANES), BF16),
            *tm_bufs((n,), ROWS),
            vm((n, CROWS, LANES), F32),
            vm((n, 2, 4, ROWS, LANES), BF16),
            vm((n, 2, 4, ROWS, LANES), BF16),
            vm((KTOT, LANES), F32),
            vm((KTOT, LANES), F32),
            vm((KTOT, LANES), BF16),
            vm((KTOT, LANES), BF16),
            vm((NZ - 1, KROWS, LANES), BF16),
            *tm_bufs((), KROWS),
            dma((7,)), dma((5,)), dma((2, 2)), dma((2, 2)),
            dma((n + 1,)), dma((n + 1,)),
            dma((n + 1, NZ - 1)), dma((n + 1, NZ - 1)),
            dma((n + 1, NZ - 1)), dma((n + 1, NZ - 1)),
            dma((n + 1, 3)), dma((n + 1, 3)),
            dma((n + 1, 3)), dma((n + 1, 3)),
            dma((n, 2, 4)), dma((n, 2, 4)),
            dma((n, 2, 4)), dma((n, 2, 4)),
            dma((n + 1, 9)), dma((n + 1, 9)),
        ],
        compiler_params=pltpu.CompilerParams(
            collective_id=0, has_side_effects=True, vmem_limit_bytes=56 << 20
        ),
        cost_estimate=pl.CostEstimate(flops=500_000_000, bytes_accessed=9_000_000, transcendentals=600_000),
        name="block_backward",
    )(
        queries.reshape(flat),
        keys.reshape(flat),
        values.reshape(flat),
        out_grad.reshape(flat),
        block_start,
        conv_input,
        conv_grad,
        conv_weight,
    )
    outs = pl.pallas_call(
        move,
        out_shape=shapes,
        in_specs=[pl.BlockSpec(memory_space=pl.ANY)] * 5,
        out_specs=[pl.BlockSpec(memory_space=pl.ANY)] * 5,
        scratch_shapes=[*[vm(o.shape, o.dtype) for o in shapes], dma((5,)), dma((5,))],
        name="results",
    )(*outs)
    shape = (frames, rows, cols, width)
    return (outs[0].reshape(shape), outs[1].reshape(shape), outs[2].reshape(shape), outs[3], outs[4])


def solution(mesh):
    split = P("tm", "space", None, None)
    return jax.shard_map(
        body,
        mesh=mesh,
        in_specs=(split, split, split, split, P("tm"), split, split, P()),
        out_specs=(split, split, split, split, P()),
        check_vma=False,
    )
```

time: 851 us -> 97.9 us (0.12)
  waiting for transfers between devices: 584 us -> 0 us
  blocking collectives: 134 us -> 0 us
  Pallas kernels: 0 us -> 97 us
  other arithmetic: 63.2 us -> 0 us
  matrix products: 28.2 us -> 0 us
  local copies, waits for them, and re-layouts: 19.3 us -> 0 us
  between operations: 14.3 us -> 0.8 us
    psum x3 -> x0, waiting for transfers between devices: 494 us -> none  [the longest x1 234 us: body(): kernel_total = lax.psum(jnp.stack(kernel_rows), ('tm', 'space'))]
    pallas_call x0 -> x2, Pallas kernels: none -> 97 us  [the longest x1 93.8 us: body(): pl.pallas_call(functools.partial(kernel, 1.0 / math.sqrt(all_tokens)), ou...]
    all_gather x2 -> x0, waiting for transfers between devices: 90.5 us -> none  [prefix(): gathered = jax.tree.map(lambda a: lax.all_gather(a, axis), part)]
    psum x2 -> x0, blocking collectives: 89.4 us -> none  [the longest x1 44.8 us: body(): states, sums = lax.psum((states, sums), 'space')]
    all_gather x2 -> x0, blocking collectives: 45 us -> none  [prefix(): gathered = jax.tree.map(lambda a: lax.all_gather(a, axis), part)]
    add x30 -> x0, other arithmetic: 33.3 us -> none  [add_pair(): return (earlier[0] + later[0], earlier[1] + later[1])]
    dot_general x12 -> x0, matrix products: 28.2 us -> none  [the longest x1 6.71 us: body(): jnp.einsum('fg,ghde->fhde', visible, states, precision=highest)]
    convert_element_type x3 -> x0, other arithmetic: 15.6 us -> none  [the longest x1 12.4 us: body(): accum.astype(jnp.bfloat16)]
  transfers between devices with their start and end apart: 7 -> 0, of which waited for: 5 -> 0; matrix products, arithmetic and copies ran while one was open for 6% -> 0% of each run, Pallas kernels for 0% -> 0%
where the time goes in v1:
time: 97.9 us; the launch traced here: 97.8 us
  Pallas kernels  97 us (99%)
    pallas_call x1, Pallas kernels, body(): pl.pallas_call(functools.partial(kernel, 1.0 / math.sqrt(all_tokens)), ou...  93.8 us
    pallas_call x1, Pallas kernels, body(): pl.pallas_call(move, out_shape=shapes, in_specs=[pl.BlockSpec(memory_spac...  3.2 us

profile of v1, /device:TPU:1, one launch (start us, length us, event | category | flops | bytes accessed | tf_op | source)
XLA Modules:
  0.0 97.8 jit_solution(10206167780256633882)
XLA Ops:
  0.6 93.8 %block_backward.1 = (bf16[128,2240]{1,0:T(8,128)(2,1)}, bf16[128,2240]{1,0:T(8,128)(2,1)}, bf16[128,2240]{1,0:T(8,128)(2,1)}, bf16[2,2,32,5632]{3,2,1,0:T(8,128)(2,1)}, f32[9,5632]{1,0:T(8,128)}) custom-call(bf16[128,2240]{1,0:T(8,128)(2,1)} %bitcast.7, bf16[128,2240]{1,0:T(8,128)(2,1)} %bitcast.8, bf16[128,2240]{1,0:T(8,128)(2,1)} %bitcast.9, ...), custom_call_target="tpu_custom_call" | custom-call | flops 500000000 | bytes 9000000 | tf_op jit(solution)/shard_map/block_backward/pallas_call | solution.py:758
  94.4 3.2 %results.1 = (bf16[128,2240]{1,0:T(8,128)(2,1)}, bf16[128,2240]{1,0:T(8,128)(2,1)}, bf16[128,2240]{1,0:T(8,128)(2,1)}, bf16[2,2,32,5632]{3,2,1,0:T(8,128)(2,1)}, f32[9,5632]{1,0:T(8,128)}) custom-call(bf16[128,2240]{1,0:T(8,128)(2,1)} %get-tuple-element.15.refs_0_, bf16[128,2240]{1,0:T(8,128)(2,1)} %get-tuple-element.16.refs_1_, ...), custom_call_target="tpu_custom_call" | custom-call | tf_op jit(solution)/shard_map/results/pallas_call | solution.py:816

commit v2 on v1

v2 whole, which is shorter than its diff:
```python
import functools
import math

import jax
import jax.numpy as jnp
from jax import lax
from jax.experimental import pallas as pl
from jax.experimental.pallas import tpu as pltpu
from jax.sharding import PartitionSpec as P

HEADS = 20
HD = 112
LANES = 128
F32 = jnp.float32
BF16 = jnp.bfloat16
MESH = pl.DeviceIdType.MESH

CHUNK_HEADS = 10
NCH = 2
NZ = 8
NR = 4
ROWS = 144
HALF = 80
CROWS = NZ * ROWS
KROWS = 96
KTOT = NZ * KROWS
KHALF = 48
TOKENS = 128
HALFTOK = 64
GROUP = 5


def lifted(wide):
    return jnp.where(wide > 0, wide + 1.0, jnp.exp(jnp.minimum(wide, 0.0)))


def dot(a, b, ca, cb):
    return lax.dot_general(a, b, (((ca,), (cb,)), ((), ())), preferred_element_type=F32)


class Place:
    def __init__(self):
        t = lax.axis_index("tm")
        s = lax.axis_index("space")
        self.t, self.s = t, s
        self.core = lax.rem(s, 2)
        self.z = lax.div(s, 2)
        self.x = lax.div(t, NR)
        self.y = lax.rem(t, NR)
        self.sibling = (t, s + 1 - 2 * self.core)
        self.up = (t, lax.rem(s + 2, 2 * NZ))
        self.down = (t, lax.rem(s + 2 * NZ - 2, 2 * NZ))
        self.ys = [(self.x * NR + lax.rem(self.y + k, NR), s) for k in (1, 2, 3)]
        self.xs = [(lax.rem(self.x + k, NR) * NR + self.y, s) for k in (1, 2, 3)]
        self.cross = (t, lax.rem(s + 2 * NZ - 1 + 2 * self.core, 2 * NZ))
        self.prev = (t, lax.rem(s + 2 * NZ - 1, 2 * NZ))
        self.next = (t, lax.rem(s + 1, 2 * NZ))


def pack(wide, step):
    lane = lax.broadcasted_iota(jnp.int32, wide.shape, 1)
    rounded = wide.astype(BF16).astype(F32)
    rest = pltpu.roll(wide - rounded, step, 1)
    return jnp.where(lane == HD + step, wide + rest, rounded).astype(BF16)


class Sum:
    forwards = 9

    def slice_from(self, d, s, far):
        o = lax.rem(self.at.z + (NZ - s if d == 0 else s), NZ)
        return self.gbuf.at[self.sl(o, *self.part(d, far))]

    def part(self, d, far):
        if not far:
            return 0, self.rows
        return (0, self.half) if d == 0 else (self.half, self.rows - self.half)

    def peer(self, d, n):
        return (self.at.t, lax.rem(self.at.s + (2 * n if d == 0 else 2 * (NZ - n)), 2 * NZ))

    def away(self, d, n):
        return lax.rem(self.at.z + (n if d == 0 else NZ - n), NZ)

    def forwarded(self, j):
        s, d = (j + 1) // 2, (j + 1) % 2
        return self.slice_from(d, s, s == 4)

    def round(self, wide):
        return wide.astype(BF16) if self.step is None else pack(wide, self.step)

    def __init__(self, at, bufs, rows, half, step):
        self.at, self.rows, self.half, self.step = at, rows, half, step
        self.pending = []
        for name, ref in bufs.items():
            setattr(self, name, ref)

    def sl(self, o, lo=0, n=None):
        n = self.rows if n is None else n
        return pl.ds(pl.multiple_of(o * self.rows + lo, 16), n)

    def remote(self, src, dst, ss, rr, dev):
        return pltpu.make_async_remote_copy(
            src_ref=src, dst_ref=dst, send_sem=ss, recv_sem=rr, device_id=dev, device_id_type=MESH
        )

    def exchange_copy(self):
        return self.remote(self.loc, self.xbuf, self.ex_s, self.ex_r, self.at.sibling)

    def go(self, make):
        make().start()
        self.pending.append(make)

    def drain(self):
        for make in self.pending:
            make().wait_send()

    def forward_copy(self, j):
        ref = self.forwarded(j)
        return self.remote(ref, ref, self.fw_s.at[j], self.fw_r.at[j], self.at.sibling)

    def finish(self):
        for j in range(self.forwards):
            self.forward_copy(j).wait_recv()


class Tree(Sum):
    def __init__(self, at, bufs, rows, half, step, mode):
        super().__init__(at, bufs, rows, half, step)
        self.mode = mode

    def far_copy(self, d, n):
        lo, count = self.part(d, n == 4)
        return self.remote(
            self.send.at[self.sl(self.away(d, n), lo, count)],
            self.recv.at[d, n - 3, pl.ds(lo, count)],
            self.rs_s.at[d, n - 3],
            self.rs_r.at[d, n - 3],
            self.peer(d, n - 2),
        )

    def near_copy(self, d):
        return self.remote(
            self.send.at[self.sl(self.away(d, 1))], self.recv.at[d, 2], self.rs_s.at[d, 2], self.rs_r.at[d, 2], self.peer(d, 1)
        )

    def middle_copy(self, d):
        return self.remote(self.middle.at[d], self.recv.at[d, 3], self.rs_s.at[d, 3], self.rs_r.at[d, 3], self.peer(d, 2))

    def scatter(self):
        self.exchange_copy().wait_recv()
        self.send[...] = self.round(self.mine[...] + self.xbuf[...])
        for n in (4, 3):
            for d in (0, 1):
                self.go(functools.partial(self.far_copy, d, n))
        for d in (0, 1):
            self.go(functools.partial(self.near_copy, d))

    def own_part(self, o, lo=0, n=None):
        at = self.sl(o, lo, n)
        return self.mine[at] + self.xbuf[at]

    def relay(self):
        for d in (0, 1):
            self.far_copy(d, 3).wait_recv()
            self.far_copy(d, 4).wait_recv()
            o = self.away(d, 2)
            lo, n = self.part(d, True)
            at = pl.ds(lo, n)
            both = self.recv[d, 0, at].astype(F32) + self.recv[d, 1, at].astype(F32)
            self.middle[d, at] = self.round(self.own_part(o, lo, n) + both)
            lo, n = self.part(1 - d, True)
            at = pl.ds(lo, n)
            self.middle[d, at] = self.round(self.own_part(o, lo, n) + self.recv[d, 0, at].astype(F32))
            self.go(functools.partial(self.middle_copy, d))

    def tm_copy(self, axis, k):
        if axis == "y":
            return self.remote(self.ysend, self.yrecv.at[k], self.y_s.at[k], self.y_r.at[k], self.at.ys[k])
        return self.remote(self.xsend, self.xrecv.at[k], self.x_s.at[k], self.x_r.at[k], self.at.xs[k])

    def weight(self, place, k):
        if self.mode == "sum":
            return 1.0
        before = (place - (k + 1) >= 0).astype(F32)
        return before if self.mode == "prefix" else 1.0 - before

    def close(self):
        own = self.own_part(self.at.z)
        for d in (0, 1):
            self.near_copy(d).wait_recv()
            own = own + self.recv[d, 2].astype(F32)
        for d in (0, 1):
            self.middle_copy(d).wait_recv()
            own = own + self.recv[d, 3].astype(F32)
        if self.mode == "lone":
            self.publish(own)
            return
        self.own[...] = own
        self.ysend[...] = self.round(own)
        for k in (1, 0, 2):
            self.go(functools.partial(self.tm_copy, "y", k))

    def over_y(self):
        total = self.own[...]
        part = total
        for k in (0, 2, 1):
            self.tm_copy("y", k).wait_recv()
            got = self.yrecv[k].astype(F32)
            total = total + got
            part = part + self.weight(self.at.y, k) * got
        self.own[...] = part
        self.xsend[...] = self.round(total)
        for k in (1, 0, 2):
            self.go(functools.partial(self.tm_copy, "x", k))

    def over_x(self):
        part = self.own[...]
        for k in (0, 2, 1):
            self.tm_copy("x", k).wait_recv()
            part = part + self.weight(self.at.x, k) * self.xrecv[k].astype(F32)
        self.publish(part)

    def publish(self, own):
        self.gbuf[self.sl(self.at.z)] = self.round(own)
        for s in (2, 1):
            for d in (0, 1):
                self.go(functools.partial(self.gather_copy, d, s))
        self.go(functools.partial(self.forward_copy, 0))

    def gather_copy(self, d, s):
        ref = self.slice_from(d, 0 if s < 3 else 2, s == 4)
        return self.remote(ref, ref, self.ag_s.at[d, s - 1], self.ag_r.at[d, s - 1], self.peer(d, s if s < 3 else s - 2))

    def arrived_copy(self, d, s):
        ref = self.slice_from(d, s, s == 4)
        return self.remote(ref, ref, self.ag_s.at[d, s - 1], self.ag_r.at[d, s - 1], self.peer(d, 1))

    def pass_on(self):
        for d in (0, 1):
            self.arrived_copy(d, 2).wait_recv()
            for s in (4, 3):
                self.go(functools.partial(self.gather_copy, d, s))
        for s in (2, 1):
            for d in (0, 1):
                if s == 1:
                    self.arrived_copy(d, 1).wait_recv()
                self.go(functools.partial(self.forward_copy, 2 * s - 1 + d))

    def gather(self):
        for s in (3, 4):
            for d in (0, 1):
                self.arrived_copy(d, s).wait_recv()
                self.go(functools.partial(self.forward_copy, 2 * s - 1 + d))


def kernel(scale, *refs):
    (
        q_hbm, k_hbm, v_hbm, g_hbm, bs_ref, ci_hbm, cg_hbm, w_hbm,
        qo, ko, vo, io, wo,
        q_in, k_in, v_in, g_in, ci_in, cg_in, w_in,
        qp, kp, vp, gp, halo, ktaps,
        loc, xbuf, gbuf,
        dsend, drecv, dmid, down, dysend, dyrecv, dxsend, dxrecv,
        kloc, kxbuf, kgbuf, ksend, krecv, kmid, kown, kysend, kyrecv, kxsend, kxrecv,
        in_sem, halo_s, halo_r,
        ex_s, ex_r, drs_s, drs_r, dag_s, dag_r, y_s, y_r, x_s, x_r,
        fw_s, fw_r,
    ) = refs
    at = Place()
    first_core, second_core = at.core == 0, at.core == 1
    channels = io.shape[-1]
    tiles = channels // LANES

    barrier = pltpu.get_barrier_semaphore()
    others = [at.sibling, at.cross, *at.ys, *at.xs]
    others += [(at.t, lax.rem(at.s + 2 * j, 2 * NZ)) for j in (1, 2, NZ - 2, NZ - 1)]
    for dev in others:
        pl.semaphore_signal(barrier, inc=1, device_id=dev, device_id_type=MESH)

    loads = [
        pltpu.make_async_copy(src, dst, in_sem.at[i])
        for i, (src, dst) in enumerate(
            [(k_hbm, k_in), (v_hbm, v_in), (q_hbm, q_in), (g_hbm, g_in), (cg_hbm, cg_in), (ci_hbm, ci_in), (w_hbm, w_in)]
        )
    ]
    for load in loads[:2]:
        load.start()

    def tree(i, which, mode):
        return Tree(
            at,
            dict(
                loc=loc.at[i, 1 - which], mine=loc.at[i, which], xbuf=xbuf.at[i], gbuf=gbuf.at[i, which],
                send=dsend.at[i], recv=drecv.at[i], middle=dmid.at[i],
                own=down.at[i], ysend=dysend.at[i], yrecv=dyrecv.at[i], xsend=dxsend.at[i], xrecv=dxrecv.at[i],
                ex_s=ex_s.at[i], ex_r=ex_r.at[i], rs_s=drs_s.at[i], rs_r=drs_r.at[i], ag_s=dag_s.at[i], ag_r=dag_r.at[i],
                y_s=y_s.at[i], y_r=y_r.at[i], x_s=x_s.at[i], x_r=x_r.at[i], fw_s=fw_s.at[i], fw_r=fw_r.at[i],
            ),
            ROWS, HALF, 2 if i < NCH else 1, mode,
        )

    pairs = [tree(i, 0, "prefix" if i < NCH else "suffix") for i in range(2 * NCH)]
    lones = [tree(i, 1, "lone") for i in range(2 * NCH)]
    i = 2 * NCH
    ksum = Tree(
        at,
        dict(
            loc=kloc, mine=kloc, xbuf=kxbuf, gbuf=kgbuf, send=ksend, recv=krecv, middle=kmid,
            own=kown, ysend=kysend, yrecv=kyrecv, xsend=kxsend, xrecv=kxrecv,
            ex_s=ex_s.at[i], ex_r=ex_r.at[i], rs_s=drs_s.at[i], rs_r=drs_r.at[i], ag_s=dag_s.at[i], ag_r=dag_r.at[i],
            y_s=y_s.at[i], y_r=y_r.at[i], x_s=x_s.at[i], x_r=x_r.at[i], fw_s=fw_s.at[i], fw_r=fw_r.at[i],
        ),
        KROWS, KHALF, None, "sum",
    )

    lane = lax.broadcasted_iota(jnp.int32, (TOKENS, LANES), 1)
    ones = ((lane == HD) | (lane == HD + 1)).astype(F32).astype(BF16)
    zero = jnp.zeros((TOKENS, LANES), BF16)

    def prepare(src, dst, heads, fill, lift):
        for h in heads:
            part = src[:, h * HD : (h + 1) * HD]
            if lift:
                part = lifted(part.astype(F32)).astype(BF16)
            dst[h] = fill
            dst[h, :, 0:HD] = part

    for i in range(2 * NCH):
        for j in range(2):
            loc[i, j, CHUNK_HEADS * HD :, :] = jnp.zeros((CROWS - CHUNK_HEADS * HD, LANES), F32)
    kloc[tiles * 16 :, :] = jnp.zeros((KTOT - tiles * 16, LANES), F32)

    @pl.when(at.s == 0)
    def _():
        halo[0] = jnp.zeros(halo.shape[1:], BF16)

    @pl.when(at.s == 2 * NZ - 1)
    def _():
        halo[1] = jnp.zeros(halo.shape[1:], BF16)

    pl.semaphore_wait(barrier, len(others))

    def halo_copy(d, f):
        return pltpu.make_async_remote_copy(
            src_ref=cg_hbm.at[f, 1 - d],
            dst_ref=halo.at[d, f],
            send_sem=halo_s.at[d, f],
            recv_sem=halo_r.at[d, f],
            device_id=at.next if d == 0 else at.prev,
            device_id_type=MESH,
        )

    has_next, has_prev = at.s < 2 * NZ - 1, at.s > 0

    def halo_start(f):
        @pl.when(has_next)
        def _():
            halo_copy(0, f).start()

        @pl.when(has_prev)
        def _():
            halo_copy(1, f).start()

    def halo_wait(f):
        @pl.when(has_prev)
        def _():
            halo_copy(0, f).wait_recv()

        @pl.when(has_next)
        def _():
            halo_copy(1, f).wait_recv()

    halo_start(0)
    loads[0].wait()
    loads[1].wait()
    for load in loads[2:]:
        load.start()

    def head_rows(h, n):
        return pl.ds(pl.multiple_of(h * HD, 16), n)

    def exchange(i):
        @pl.when(first_core)
        def _():
            pairs[i].exchange_copy().start()

        @pl.when(second_core)
        def _():
            lones[i].exchange_copy().start()

    def states(c):
        def some(n, _):
            heads = [n * GROUP + u for u in range(GROUP)]
            ks = [kp[c * CHUNK_HEADS + h] for h in heads]
            vs = [vp[c * CHUNK_HEADS + h] for h in heads]
            both = [dot(k, v, 0, 0)[:HD] for k, v in zip(ks, vs)]
            lone = [dot(k[HALFTOK:], v[HALFTOK:], 0, 0)[:HD] for k, v in zip(ks, vs)]
            for h, b, l in zip(heads, both, lone):
                loc[c, 0, head_rows(h, HD)] = b
                loc[c, 1, head_rows(h, HD)] = l
            return 0

        lax.fori_loop(0, CHUNK_HEADS // GROUP, some, 0)
        exchange(c)

    chunk = [range(c * CHUNK_HEADS, (c + 1) * CHUNK_HEADS) for c in range(NCH)]
    for c in range(NCH):
        prepare(k_in, kp, chunk[c], zero, True)
        prepare(v_in, vp, chunk[c], ones, False)
        states(c)

    col = lax.broadcasted_iota(jnp.int32, (32, LANES), 0)
    not_first, not_last = col > 0, col < 31

    def conv_tile(f, n, _):
        at_lane = pl.ds(pl.multiple_of(n * LANES, LANES), LANES)
        taps = [w_in[t : t + 1, at_lane] for t in range(9)]
        sums9 = [None] * 9
        rows = [halo[0, f, :, at_lane], cg_in[f, 0, :, at_lane], cg_in[f, 1, :, at_lane], halo[1, f, :, at_lane]]
        outs = [None, None]
        inner = [ci_in[f, r, :, at_lane].astype(F32) for r in range(2)]
        for m in range(4):
            wide = rows[m].astype(F32)
            later = jnp.where(not_last, pltpu.roll(wide, 31, 0), 0.0)
            earlier = jnp.where(not_first, pltpu.roll(wide, 1, 0), 0.0)
            for r in range(2):
                i = r + 2 - m
                if 0 <= i <= 2:
                    for j, window in enumerate((later, wide, earlier)):
                        t = 3 * i + j
                        add = taps[t] * window
                        outs[r] = add if outs[r] is None else outs[r] + add
                        prod = window * inner[r]
                        prod = prod[0:8] + prod[8:16] + (prod[16:24] + prod[24:32])
                        sums9[t] = prod if sums9[t] is None else sums9[t] + prod
        for r in range(2):
            io[f, r, :, at_lane] = outs[r].astype(BF16)
        total = jnp.concatenate(
            [jnp.sum(a, axis=0, keepdims=True) for a in sums9] + [jnp.zeros((7, LANES), F32)], axis=0
        )
        place = pl.ds(pl.multiple_of(n * 16, 16), 16)
        if f == 0:
            ktaps[place] = total
        else:
            kloc[place] = ktaps[place] + total
        return 0

    def conv(f, a, b):
        lax.fori_loop(a, b, functools.partial(conv_tile, f), 0)

    bs = bs_ref[1].astype(F32)

    def queries(c, n):
        lanes = lane[:HALFTOK]

        def some(n, _):
            heads = [n * GROUP + u for u in range(GROUP)]
            whole = [(qp[c * CHUNK_HEADS + h], gp[c * CHUNK_HEADS + h]) for h in heads]
            states = []
            for h in heads:
                last = gbuf[c, 0, head_rows(h, LANES)]
                lone = gbuf[c, 1, head_rows(h, LANES)]
                states.append((pack(last.astype(F32) - bs * lone.astype(F32), 2), last))
            parts = [
                (q[f * HALFTOK : (f + 1) * HALFTOK], g[f * HALFTOK : (f + 1) * HALFTOK].astype(F32), s[f])
                for (q, g), s in zip(whole, states)
                for f in range(2)
            ]
            numers = [dot(q, s, 1, 0) for q, _, s in parts]
            dns = []
            for (_, g, _), numer in zip(parts, numers):
                inv = 1.0 / (numer[:, HD : HD + 1] + numer[:, HD + 2 : HD + 3])
                dd = -(jnp.sum(g * numer, axis=1, keepdims=True) * inv) * inv
                hi = dd.astype(BF16).astype(F32)
                wide = jnp.where((lanes == HD) | (lanes == HD + 2), hi, g * inv)
                dns.append(jnp.where(lanes == HD + 1, dd - hi, wide).astype(BF16))
            grads = [
                (dot(dn, s, 1, 1) * jnp.minimum(q.astype(F32), 1.0)).astype(BF16) for (q, _, s), dn in zip(parts, dns)
            ]
            both = [
                dot(q, jnp.concatenate(dns[2 * u : 2 * u + 2], axis=0), 0, 0)[:HD] for u, (q, _) in enumerate(whole)
            ]
            lone = [dot(parts[2 * u][0], dns[2 * u], 0, 0)[:HD] for u in range(GROUP)]
            for u, h in enumerate(heads):
                loc[NCH + c, 0, head_rows(h, HD)] = both[u]
                loc[NCH + c, 1, head_rows(h, HD)] = lone[u]
                gp[c * CHUNK_HEADS + h] = jnp.concatenate(grads[2 * u : 2 * u + 2], axis=0)
            return 0

        lax.fori_loop(n, n + 1, some, 0)
        if n == CHUNK_HEADS // GROUP - 1:
            exchange(NCH + c)

    def keys(c):
        def some(n, _):
            heads = [n * GROUP + u for u in range(GROUP)]
            whole = [(kp[c * CHUNK_HEADS + h], vp[c * CHUNK_HEADS + h]) for h in heads]
            states = []
            for h in heads:
                first = gbuf[NCH + c, 0, head_rows(h, LANES)]
                lone = gbuf[NCH + c, 1, head_rows(h, LANES)]
                states.append((first, pack(first.astype(F32) - bs * lone.astype(F32), 1)))
            outs = []
            for (k, v), s in zip(whole, states):
                kg = jnp.concatenate(
                    [dot(v[f * HALFTOK : (f + 1) * HALFTOK], s[f], 1, 1) for f in range(2)], axis=0
                )
                vg = jnp.concatenate(
                    [dot(k[f * HALFTOK : (f + 1) * HALFTOK], s[f], 1, 0) for f in range(2)], axis=0
                )
                outs.append(((kg * jnp.minimum(k.astype(F32), 1.0)).astype(BF16), vg.astype(BF16)))
            for h, (kg, vg) in zip(heads, outs):
                kp[c * CHUNK_HEADS + h] = kg
                vp[c * CHUNK_HEADS + h] = vg
            return 0

        lax.fori_loop(0, CHUNK_HEADS // GROUP, some, 0)

    def write(src, dst, heads):
        for h in heads:
            dst[:, h * HD : (h + 1) * HD] = src[h, :, 0:HD]

    def prepare_queries():
        loads[2].wait()
        loads[3].wait()
        for c in range(NCH):
            prepare(q_in, qp, chunk[c], zero, True)
            prepare(g_in, gp, chunk[c], zero, False)

    def conv_loads():
        for n in (4, 5, 6):
            loads[n].wait()

    half = tiles // 2

    @pl.when(first_core)
    def _():
        a, b = pairs[0], pairs[1]
        a.scatter()
        b.scatter()
        prepare_queries()
        a.relay()
        b.relay()
        a.close()
        b.close()
        halo_start(1)
        conv_loads()
        halo_wait(0)
        conv(0, 0, half)
        a.over_y()
        b.over_y()
        conv(0, half, tiles)
        a.over_x()
        b.over_x()
        a.pass_on()
        b.pass_on()
        halo_wait(1)
        conv(1, 0, half)
        a.gather()

    @pl.when(second_core)
    def _():
        a, b = lones[0], lones[1]
        prepare_queries()
        a.scatter()
        b.scatter()
        conv_loads()
        a.relay()
        b.relay()
        halo_start(1)
        a.close()
        b.close()
        halo_wait(0)
        conv(0, 0, half)
        a.pass_on()
        b.pass_on()
        conv(0, half, tiles)
        a.gather()
        b.gather()
        halo_wait(1)
        conv(1, 0, tiles)

    def finish(i):
        @pl.when(first_core)
        def _():
            lones[i].finish()

        @pl.when(second_core)
        def _():
            pairs[i].finish()

    finish(0)
    queries(0, 0)
    pl.when(first_core)(pairs[1].gather)
    queries(0, 1)
    finish(1)
    queries(1, 0)
    pl.when(first_core)(pairs[NCH].scatter)
    queries(1, 1)

    @pl.when(first_core)
    def _():
        a, b = pairs[NCH], pairs[NCH + 1]
        b.scatter()
        conv(1, half, tiles)
        ksum.exchange_copy().start()
        a.relay()
        b.relay()
        a.close()
        b.close()
        write(gp, qo, chunk[0])
        a.over_y()
        b.over_y()
        write(gp, qo, chunk[1])
        a.over_x()
        b.over_x()
        a.pass_on()
        b.pass_on()
        a.gather()

    @pl.when(second_core)
    def _():
        a, b = lones[NCH], lones[NCH + 1]
        write(gp, qo, chunk[0])
        write(gp, qo, chunk[1])
        a.scatter()
        b.scatter()
        a.relay()
        b.relay()
        ksum.scatter()
        a.close()
        b.close()
        ksum.relay()
        a.pass_on()
        b.pass_on()
        ksum.close()
        a.gather()
        b.gather()
        ksum.over_y()
        ksum.over_x()
        ksum.pass_on()

    for c in range(NCH):
        finish(NCH + c)
        keys(c)
        if c == 0:
            pl.when(first_core)(pairs[NCH + 1].gather)
            pl.when(second_core)(ksum.gather)
        write(kp, ko, chunk[c])
        write(vp, vo, chunk[c])

    @pl.when(first_core)
    def _():
        ksum.finish()

    for n in range(tiles):
        wo[:, n * LANES : (n + 1) * LANES] = kgbuf[n * 16 : n * 16 + 16].astype(F32)[:9] * scale

    @pl.when(first_core)
    def _():
        for s in pairs:
            s.exchange_copy().wait_send()
            s.drain()
        ksum.exchange_copy().wait_send()

    @pl.when(second_core)
    def _():
        for s in lones:
            s.exchange_copy().wait_send()
            s.drain()
        ksum.drain()

    for f in range(2):

        @pl.when(has_next)
        def _():
            halo_copy(0, f).wait_send()

        @pl.when(has_prev)
        def _():
            halo_copy(1, f).wait_send()


def move(*refs):
    srcs, dsts, sem = refs[:5], refs[5:10], refs[10]
    copies = [pltpu.make_async_copy(s, d, sem.at[i]) for i, (s, d) in enumerate(zip(srcs, dsts))]
    for copy in copies:
        copy.start()
    for copy in copies:
        copy.wait()


def body(queries, keys, values, out_grad, block_start, conv_input, conv_grad, conv_weight):
    frames, rows, cols, width = queries.shape
    channels = conv_grad.shape[-1]
    tokens = frames * rows * cols
    all_tokens = tokens * lax.axis_size("tm") * lax.axis_size("space")
    flat = (tokens, width)
    conv_shape = conv_grad.shape
    n = 2 * NCH
    vm, dma = pltpu.VMEM, pltpu.SemaphoreType.DMA

    def tm_bufs(lead, rows_):
        return [
            vm((*lead, rows_, LANES), F32),
            vm((*lead, rows_, LANES), BF16),
            vm((*lead, 3, rows_, LANES), BF16),
            vm((*lead, rows_, LANES), BF16),
            vm((*lead, 3, rows_, LANES), BF16),
        ]

    shapes = (
        jax.ShapeDtypeStruct(flat, BF16),
        jax.ShapeDtypeStruct(flat, BF16),
        jax.ShapeDtypeStruct(flat, BF16),
        jax.ShapeDtypeStruct(conv_shape, BF16),
        jax.ShapeDtypeStruct(conv_weight.shape, F32),
    )
    outs = pl.pallas_call(
        functools.partial(kernel, 1.0 / math.sqrt(all_tokens)),
        out_shape=[pltpu.VMEM(o.shape, o.dtype) for o in shapes],
        in_specs=[pl.BlockSpec(memory_space=pl.ANY)] * 4
        + [pl.BlockSpec(memory_space=pltpu.SMEM)]
        + [pl.BlockSpec(memory_space=pl.ANY)] * 3,
        out_specs=[pl.BlockSpec(memory_space=pltpu.VMEM)] * 5,
        scratch_shapes=[
            *[vm(flat, BF16)] * 4,
            vm(conv_shape, BF16),
            vm(conv_shape, BF16),
            vm(conv_weight.shape, F32),
            *[vm((HEADS, tokens, LANES), BF16)] * 4,
            vm((2, frames, cols, channels), BF16),
            vm((KTOT, LANES), F32),
            vm((n, 2, CROWS, LANES), F32),
            vm((n, CROWS, LANES), F32),
            vm((n, 2, CROWS, LANES), BF16),
            vm((n, CROWS, LANES), BF16),
            vm((n, 2, 4, ROWS, LANES), BF16),
            vm((n, 2, ROWS, LANES), BF16),
            *tm_bufs((n,), ROWS),
            vm((KTOT, LANES), F32),
            vm((KTOT, LANES), F32),
            vm((KTOT, LANES), BF16),
            vm((KTOT, LANES), BF16),
            vm((2, 4, KROWS, LANES), BF16),
            vm((2, KROWS, LANES), BF16),
            *tm_bufs((), KROWS),
            dma((7,)), dma((2, 2)), dma((2, 2)),
            dma((n + 1,)), dma((n + 1,)),
            dma((n + 1, 2, 4)), dma((n + 1, 2, 4)),
            dma((n + 1, 2, 4)), dma((n + 1, 2, 4)),
            dma((n + 1, 3)), dma((n + 1, 3)),
            dma((n + 1, 3)), dma((n + 1, 3)),
            dma((n + 1, 9)), dma((n + 1, 9)),
        ],
        compiler_params=pltpu.CompilerParams(
            collective_id=0, has_side_effects=True, vmem_limit_bytes=56 << 20
        ),
        cost_estimate=pl.CostEstimate(flops=500_000_000, bytes_accessed=9_000_000, transcendentals=600_000),
        name="block_backward",
    )(
        queries.reshape(flat),
        keys.reshape(flat),
        values.reshape(flat),
        out_grad.reshape(flat),
        block_start,
        conv_input,
        conv_grad,
        conv_weight,
    )
    outs = pl.pallas_call(
        move,
        out_shape=shapes,
        in_specs=[pl.BlockSpec(memory_space=pltpu.VMEM)] * 5,
        out_specs=[pl.BlockSpec(memory_space=pl.ANY)] * 5,
        scratch_shapes=[dma((5,))],
        compiler_params=pltpu.CompilerParams(vmem_limit_bytes=1 << 20),
        name="results",
    )(*outs)
    shape = (frames, rows, cols, width)
    return (outs[0].reshape(shape), outs[1].reshape(shape), outs[2].reshape(shape), outs[3], outs[4])


def solution(mesh):
    split = P("tm", "space", None, None)
    return jax.shard_map(
        body,
        mesh=mesh,
        in_specs=(split, split, split, split, P("tm"), split, split, P()),
        out_specs=(split, split, split, split, P()),
        check_vma=False,
    )
```

time: 97.9 us -> 82.9 us (0.85)
  Pallas kernels: 97 us -> 82 us
    pallas_call x1, Pallas kernels: 93.8 us -> 80.1 us  [body(): pl.pallas_call(functools.partial(kernel, 1.0 / math.sqrt(all_tokens)), ou...]
    pallas_call x1, Pallas kernels: 3.2 us -> 1.84 us  [body(): pl.pallas_call(move, out_shape=shapes, in_specs=[pl.BlockSpec(memory_spac...]
where the time goes in v2:
time: 82.9 us; the launch traced here: 82.8 us
  Pallas kernels  82 us (99%)
    pallas_call x1, Pallas kernels, body(): pl.pallas_call(functools.partial(kernel, 1.0 / math.sqrt(all_tokens)), ou...  80.1 us
    pallas_call x1, Pallas kernels, body(): pl.pallas_call(move, out_shape=shapes, in_specs=[pl.BlockSpec(memory_spac...  1.84 us

profile of v2, /device:TPU:1, one launch (start us, length us, event | category | flops | bytes accessed | tf_op | source)
XLA Modules:
  0.0 82.8 jit_solution(12691948872027809081)
XLA Ops:
  0.6 80.1 %block_backward.1 = (bf16[128,2240]{1,0:T(8,128)(2,1)S(1)}, bf16[128,2240]{1,0:T(8,128)(2,1)S(1)}, bf16[128,2240]{1,0:T(8,128)(2,1)S(1)}, bf16[2,2,32,5632]{3,2,1,0:T(8,128)(2,1)S(1)}, f32[9,5632]{1,0:T(8,128)S(1)}) custom-call(bf16[128,2240]{1,0:T(8,128)(2,1)} %bitcast.7, bf16[128,2240]{1,0:T(8,128)(2,1)} %bitcast.8, bf16[128,2240]{1,0:T(8,128)(2,1)} %bitcast.9, ...), custom_call_target="tpu_custom_call" | custom-call | flops 500000000 | bytes 9000000 | tf_op jit(solution)/shard_map/block_backward/pallas_call | solution.py:720
  80.8 1.8 %results.1 = (bf16[128,2240]{1,0:T(8,128)(2,1)}, bf16[128,2240]{1,0:T(8,128)(2,1)}, bf16[128,2240]{1,0:T(8,128)(2,1)}, bf16[2,2,32,5632]{3,2,1,0:T(8,128)(2,1)}, f32[9,5632]{1,0:T(8,128)}) custom-call(bf16[128,2240]{1,0:T(8,128)(2,1)S(1)} %get-tuple-element.15.refs_0_, bf16[128,2240]{1,0:T(8,128)(2,1)S(1)} %get-tuple-element.16.refs_1_, ...), custom_call_target="tpu_custom_call" | custom-call | tf_op jit(solution)/shard_map/results/pallas_call | solution.py:772

commit v3 on v2

--- a/solution.py
+++ b/solution.py
@@ -339,8 +339,6 @@
     def _():
         halo[1] = jnp.zeros(halo.shape[1:], BF16)
 
-    pl.semaphore_wait(barrier, len(others))
-
     def halo_copy(d, f):
         return pltpu.make_async_remote_copy(
             src_ref=cg_hbm.at[f, 1 - d],
@@ -371,7 +369,6 @@
         def _():
             halo_copy(1, f).wait_recv()
 
-    halo_start(0)
     loads[0].wait()
     loads[1].wait()
     for load in loads[2:]:
@@ -394,11 +391,12 @@
             heads = [n * GROUP + u for u in range(GROUP)]
             ks = [kp[c * CHUNK_HEADS + h] for h in heads]
             vs = [vp[c * CHUNK_HEADS + h] for h in heads]
-            both = [dot(k, v, 0, 0)[:HD] for k, v in zip(ks, vs)]
-            lone = [dot(k[HALFTOK:], v[HALFTOK:], 0, 0)[:HD] for k, v in zip(ks, vs)]
-            for h, b, l in zip(heads, both, lone):
-                loc[c, 0, head_rows(h, HD)] = b
-                loc[c, 1, head_rows(h, HD)] = l
+            empty = jnp.zeros((HALFTOK, LANES), BF16)
+            wide = [jnp.concatenate([v, jnp.concatenate([empty, v[HALFTOK:]], axis=0)], axis=1) for v in vs]
+            outs = [dot(k, w, 0, 0)[:HD] for k, w in zip(ks, wide)]
+            for h, o in zip(heads, outs):
+                loc[c, 0, head_rows(h, HD)] = o[:, :LANES]
+                loc[c, 1, head_rows(h, HD)] = o[:, LANES:]
             return 0
 
         lax.fori_loop(0, CHUNK_HEADS // GROUP, some, 0)
@@ -408,6 +406,9 @@
     for c in range(NCH):
         prepare(k_in, kp, chunk[c], zero, True)
         prepare(v_in, vp, chunk[c], ones, False)
+        if c == 0:
+            pl.semaphore_wait(barrier, len(others))
+            halo_start(0)
         states(c)
 
     col = lax.broadcasted_iota(jnp.int32, (32, LANES), 0)
@@ -478,13 +479,21 @@
             grads = [
                 (dot(dn, s, 1, 1) * jnp.minimum(q.astype(F32), 1.0)).astype(BF16) for (q, _, s), dn in zip(parts, dns)
             ]
-            both = [
-                dot(q, jnp.concatenate(dns[2 * u : 2 * u + 2], axis=0), 0, 0)[:HD] for u, (q, _) in enumerate(whole)
+            empty = jnp.zeros((HALFTOK, LANES), BF16)
+            wide = [
+                jnp.concatenate(
+                    [
+                        jnp.concatenate(dns[2 * u : 2 * u + 2], axis=0),
+                        jnp.concatenate([dns[2 * u], empty], axis=0),
+                    ],
+                    axis=1,
+                )
+                for u in range(GROUP)
             ]
-            lone = [dot(parts[2 * u][0], dns[2 * u], 0, 0)[:HD] for u in range(GROUP)]
+            outs = [dot(q, w, 0, 0)[:HD] for (q, _), w in zip(whole, wide)]
             for u, h in enumerate(heads):
-                loc[NCH + c, 0, head_rows(h, HD)] = both[u]
-                loc[NCH + c, 1, head_rows(h, HD)] = lone[u]
+                loc[NCH + c, 0, head_rows(h, HD)] = outs[u][:, :LANES]
+                loc[NCH + c, 1, head_rows(h, HD)] = outs[u][:, LANES:]
                 gp[c * CHUNK_HEADS + h] = jnp.concatenate(grads[2 * u : 2 * u + 2], axis=0)
             return 0
 
@@ -555,8 +564,6 @@
         b.over_x()
         a.pass_on()
         b.pass_on()
-        halo_wait(1)
-        conv(1, 0, half)
         a.gather()
 
     @pl.when(second_core)
@@ -602,11 +609,14 @@
     @pl.when(first_core)
     def _():
         a, b = pairs[NCH], pairs[NCH + 1]
+        halo_wait(1)
+        conv(1, 0, tiles // 4)
         b.scatter()
+        a.relay()
+        conv(1, tiles // 4, half)
+        b.relay()
         conv(1, half, tiles)
         ksum.exchange_copy().start()
-        a.relay()
-        b.relay()
         a.close()
         b.close()
         write(gp, qo, chunk[0])

time: 82.9 us -> 82.6 us (level)
  no operation moved by 1% of the time
where the time goes in v3:
time: 82.6 us; the launch traced here: 82.5 us
  Pallas kernels  81.7 us (99%)
    pallas_call x1, Pallas kernels, body(): pl.pallas_call(functools.partial(kernel, 1.0 / math.sqrt(all_tokens)), ou...  79.8 us
    pallas_call x1, Pallas kernels, body(): pl.pallas_call(move, out_shape=shapes, in_specs=[pl.BlockSpec(memory_spac...  1.84 us

profile of v3, /device:TPU:1, one launch (start us, length us, event | category | flops | bytes accessed | tf_op | source)
XLA Modules:
  0.0 82.5 jit_solution(16382701975653525461)
XLA Ops:
  0.6 79.8 %block_backward.1 = (bf16[128,2240]{1,0:T(8,128)(2,1)S(1)}, bf16[128,2240]{1,0:T(8,128)(2,1)S(1)}, bf16[128,2240]{1,0:T(8,128)(2,1)S(1)}, bf16[2,2,32,5632]{3,2,1,0:T(8,128)(2,1)S(1)}, f32[9,5632]{1,0:T(8,128)S(1)}) custom-call(bf16[128,2240]{1,0:T(8,128)(2,1)} %bitcast.7, bf16[128,2240]{1,0:T(8,128)(2,1)} %bitcast.8, bf16[128,2240]{1,0:T(8,128)(2,1)} %bitcast.9, ...), custom_call_target="tpu_custom_call" | custom-call | flops 500000000 | bytes 9000000 | tf_op jit(solution)/shard_map/block_backward/pallas_call | solution.py:730
  80.5 1.8 %results.1 = (bf16[128,2240]{1,0:T(8,128)(2,1)}, bf16[128,2240]{1,0:T(8,128)(2,1)}, bf16[128,2240]{1,0:T(8,128)(2,1)}, bf16[2,2,32,5632]{3,2,1,0:T(8,128)(2,1)}, f32[9,5632]{1,0:T(8,128)}) custom-call(bf16[128,2240]{1,0:T(8,128)(2,1)S(1)} %get-tuple-element.15.refs_0_, bf16[128,2240]{1,0:T(8,128)(2,1)S(1)} %get-tuple-element.16.refs_1_, ...), custom_call_target="tpu_custom_call" | custom-call | tf_op jit(solution)/shard_map/results/pallas_call | solution.py:782
